TPU v7x, 128 devices: a whole 4x4x4 slice. The times are simulated.
128 devices in a mesh: pts: 8 (over x, core), ca: 4 (over y), cb: 4 (over z).
Axes of the slice: x: 4, y: 4, z: 4, core: 2. Of those that a mesh axis runs over, the one named last changes fastest.
Arguments:
- points: bfloat16 [131072, 1024], P(('pts', 'ca', 'cb')), may hold values from -6 to 6
- candidates: bfloat16 [12288, 1024], P(('ca', 'cb')), may hold values from -0.1875 to 0.1875
- probes: int32 [1024, 24], P(('pts', 'ca', 'cb')), may hold values from 0 to 95, all different within a row
- chosen: int32 [4], replicated, may hold values from 0 to 12287
Outputs:
- facility_gains: float32 [4, 12288], P(None, ('ca', 'cb'))
- coverage: float32 [131072], P(('pts', 'ca', 'cb'))
Inputs may be any that keep to these rules, and one draw needn't show every extreme that they name: `probes`: the 24 entries of a row are distinct; every candidate block is probed by some point block.
All inputs are finite; a program needn't handle non-finite values.
Results may differ from a plain program's by a relative error of at most 0.0003.
Values may be sent and summed in bfloat16 or wider, within the bound.
A program may use at most 128 MiB of HBM per device.

v0:
```python
import jax
import jax.numpy as jnp
from jax import lax
from jax.sharding import PartitionSpec as P

BLK = 128
PROBES = 24
STEPS = 4


def before_of(point_rows, facility):
    facility_sim = jnp.dot(point_rows, facility.T, preferred_element_type=jnp.float32)
    covered = jnp.zeros((point_rows.shape[0],), jnp.float32)
    columns = []
    for round_index in range(STEPS):
        columns.append(covered)
        covered = jnp.maximum(covered, facility_sim[:, round_index])
    return (jnp.stack(columns, axis=1), covered)


def local(points, candidates, probes, chosen):
    feature = points.shape[1]
    own_rows = candidates.shape[0]
    owner_start = lax.axis_index(("ca", "cb")) * own_rows
    local_id = chosen - owner_start
    inside = (local_id >= 0) & (local_id < own_rows)
    picked = jnp.take(candidates, jnp.clip(local_id, 0, own_rows - 1), axis=0).astype(jnp.float32)
    mine = jnp.where(inside[:, None], picked, 0.0)
    facility = lax.psum(mine, ("ca", "cb")).astype(jnp.bfloat16)
    before, coverage = before_of(points, facility)
    dims = (((1,), (1,)), ((), ()))
    gathered = lax.all_gather(candidates, ("ca", "cb"), axis=0, tiled=True)
    cand_blocks = gathered.reshape(-1, BLK, feature)
    cand_count = cand_blocks.shape[0]
    labels = jnp.arange(cand_count, dtype=jnp.int32)

    def add_block(running, inputs):
        point_rows, probe_row, before_rows = inputs
        taken = jnp.take(cand_blocks, probe_row, axis=0).reshape(PROBES * BLK, feature)
        similar = lax.dot_general(point_rows, taken, dims, preferred_element_type=jnp.float32)
        contrib = jnp.maximum(similar[None, :, :] - before_rows.T[:, :, None], 0.0)
        summed = jnp.sum(contrib, axis=1).reshape(STEPS, PROBES, BLK)
        onehot = (probe_row[:, None] == labels[None, :]).astype(jnp.float32)
        added = jnp.einsum("spr,pc->scr", summed, onehot, precision=lax.Precision.HIGHEST)
        return (running + added, None)

    start_blocks = jnp.zeros((STEPS, cand_count, BLK), jnp.float32)
    inputs = (points.reshape(-1, BLK, feature), probes, before.reshape(-1, BLK, STEPS))
    running, _ = lax.scan(add_block, start_blocks, inputs)
    partial_gains = running.reshape(STEPS, cand_count * BLK)
    shares = lax.psum_scatter(partial_gains, ("ca", "cb"), scatter_dimension=1, tiled=True)
    totals = lax.psum(shares, "pts")
    return (totals / (BLK * PROBES), coverage)


def solution(mesh):
    return jax.shard_map(
        local,
        mesh=mesh,
        in_specs=(
            P(("pts", "ca", "cb"), None),
            P(("ca", "cb"), None),
            P(("pts", "ca", "cb"), None),
            P(),
        ),
        out_specs=(P(None, ("ca", "cb")), P(("pts", "ca", "cb"))),
        check_vma=False,
    )
```

profile of v0, /device:TPU:1, one launch (start us, length us, event | category | flops | bytes accessed | tf_op | source)
XLA Modules:
  0.0 458.8 jit_solution(365145382629259075)
XLA Ops:
  8.6 2.2 gather_fusion.1
  10.9 63.6 %psum.14 = bf16[4,1024]{1,0:T(4,128)(2,1)S(1)} all-reduce(f32[4,1024]{1,0:T(4,128)S(1)} %convert_select_fusion), channel_id=1, replica_groups=mesh['pts'=8,'ca'=4,'cb'=4] {'ca','cb'}, use_global_device_ids=true, to_apply=%region_0.1 | all-reduce | flops 4096 | bytes 24576 | tf_op jit(solution)/shard_map/psum | solution.py:29
  74.5 2.2 convolution_bitcast_fusion.1
  77.4 91.3 %all-gather.2.cloned.1.call-done = bf16[12288,1024]{1,0:T(8,128)(2,1)} async-done(((bf16[768,1024]{1,0:T(8,128)(2,1)}), bf16[12288,1024]{1,0:T(8,128)(2,1)}) %all-gather.2.cloned.1.call-update) | async-done | bytes 25165840 | tf_op jit(solution)/shard_map/all_gather | solution.py:32
  168.7 174.9 %while.11 = (s32[]{:T(128)}, f32[4,96,128]{2,1,0:T(8,128)S(1)}, s32[8,24]{1,0:T(8,128)}, bf16[8,128,1024]{2,1,0:T(8,128)(2,1)}, bf16[96,128,1024]{2,1,0:T(8,128)...) while((s32[]{:T(128)}, f32[4,96,128]{2,1,0:T(8,128)S(1)}, s32[8,24]{1,0:T(8,128)}, ...), condition=%wide.region_3.4_spmd.clone, body=%wide.region_1.3_spmd.clone.sunk | while | flops 827416000 | bytes 35368248 | solution.py:49
  169.4 12.7 %gather_fusion = bf16[24,128,1024]{2,1,0:T(8,128)(2,1)} fusion(bf16[96,128,1024]{2,1,0:T(8,128)(2,1)} %get-tuple-element.145, s32[1024]{0:T(1024)S(1)} %pad_clamp_fusion.3), kind=kCustom, calls=%fused_computation.clone.clone.1 | custom fusion | bytes 12583008 | tf_op jit(solution)/shard_map/while/body/eval_jaxpr/jit(_take)/gather | solution.py:39
  182.8 3.4 broadcast_select_fusion.2
  186.2 3.1 fusion.33
  189.4 0.8 maximum_reduce_fusion.2
  190.6 0.7 fusion.32
  191.3 12.7 %gather_fusion = bf16[24,128,1024]{2,1,0:T(8,128)(2,1)} fusion(bf16[96,128,1024]{2,1,0:T(8,128)(2,1)} %get-tuple-element.145, s32[1024]{0:T(1024)S(1)} %pad_clamp_fusion.3), kind=kCustom, calls=%fused_computation.clone.clone.1 | custom fusion | bytes 12583008 | tf_op jit(solution)/shard_map/while/body/eval_jaxpr/jit(_take)/gather | solution.py:39
  204.7 3.4 broadcast_select_fusion.2
  208.1 3.2 fusion.33
  211.3 0.8 maximum_reduce_fusion.2
  212.5 0.7 fusion.32
  213.2 12.7 %gather_fusion = bf16[24,128,1024]{2,1,0:T(8,128)(2,1)} fusion(bf16[96,128,1024]{2,1,0:T(8,128)(2,1)} %get-tuple-element.145, s32[1024]{0:T(1024)S(1)} %pad_clamp_fusion.3), kind=kCustom, calls=%fused_computation.clone.clone.1 | custom fusion | bytes 12583008 | tf_op jit(solution)/shard_map/while/body/eval_jaxpr/jit(_take)/gather | solution.py:39
  226.5 3.4 broadcast_select_fusion.2
  230.0 3.2 fusion.33
  233.2 0.8 maximum_reduce_fusion.2
  234.3 0.7 fusion.32
  235.1 12.6 %gather_fusion = bf16[24,128,1024]{2,1,0:T(8,128)(2,1)} fusion(bf16[96,128,1024]{2,1,0:T(8,128)(2,1)} %get-tuple-element.145, s32[1024]{0:T(1024)S(1)} %pad_clamp_fusion.3), kind=kCustom, calls=%fused_computation.clone.clone.1 | custom fusion | bytes 12583008 | tf_op jit(solution)/shard_map/while/body/eval_jaxpr/jit(_take)/gather | solution.py:39
  248.4 3.4 broadcast_select_fusion.2
  251.9 3.1 fusion.33
  255.0 0.8 maximum_reduce_fusion.2
  256.2 0.7 fusion.32
  256.9 12.7 %gather_fusion = bf16[24,128,1024]{2,1,0:T(8,128)(2,1)} fusion(bf16[96,128,1024]{2,1,0:T(8,128)(2,1)} %get-tuple-element.145, s32[1024]{0:T(1024)S(1)} %pad_clamp_fusion.3), kind=kCustom, calls=%fused_computation.clone.clone.1 | custom fusion | bytes 12583008 | tf_op jit(solution)/shard_map/while/body/eval_jaxpr/jit(_take)/gather | solution.py:39
  270.3 3.4 broadcast_select_fusion.2
  273.7 3.2 fusion.33
  276.9 0.8 maximum_reduce_fusion.2
  278.1 0.7 fusion.32
  278.8 12.7 %gather_fusion = bf16[24,128,1024]{2,1,0:T(8,128)(2,1)} fusion(bf16[96,128,1024]{2,1,0:T(8,128)(2,1)} %get-tuple-element.145, s32[1024]{0:T(1024)S(1)} %pad_clamp_fusion.3), kind=kCustom, calls=%fused_computation.clone.clone.1 | custom fusion | bytes 12583008 | tf_op jit(solution)/shard_map/while/body/eval_jaxpr/jit(_take)/gather | solution.py:39
  292.1 3.4 broadcast_select_fusion.2
  295.6 3.2 fusion.33
  298.8 0.8 maximum_reduce_fusion.2
  300.0 0.7 fusion.32
  300.7 12.7 %gather_fusion = bf16[24,128,1024]{2,1,0:T(8,128)(2,1)} fusion(bf16[96,128,1024]{2,1,0:T(8,128)(2,1)} %get-tuple-element.145, s32[1024]{0:T(1024)S(1)} %pad_clamp_fusion.3), kind=kCustom, calls=%fused_computation.clone.clone.1 | custom fusion | bytes 12583008 | tf_op jit(solution)/shard_map/while/body/eval_jaxpr/jit(_take)/gather | solution.py:39
  314.0 3.4 broadcast_select_fusion.2
  317.5 3.2 fusion.33
  320.7 0.8 maximum_reduce_fusion.2
  321.8 0.7 fusion.32
  322.5 12.6 %gather_fusion = bf16[24,128,1024]{2,1,0:T(8,128)(2,1)} fusion(bf16[96,128,1024]{2,1,0:T(8,128)(2,1)} %get-tuple-element.145, s32[1024]{0:T(1024)S(1)} %pad_clamp_fusion.3), kind=kCustom, calls=%fused_computation.clone.clone.1 | custom fusion | bytes 12583008 | tf_op jit(solution)/shard_map/while/body/eval_jaxpr/jit(_take)/gather | solution.py:39
  335.9 3.4 broadcast_select_fusion.2
  339.3 3.1 fusion.33
  342.5 0.8 maximum_reduce_fusion.2
  343.7 4.0 copy.17
  347.7 79.8 %reduce-scatter.4.cloned.1.call-done = f32[768,4]{1,0:T(8,128)} async-done(((f32[12288,4]{1,0:T(8,128)}), f32[768,4]{1,0:T(8,128)}) %reduce-scatter.4.cloned.1.call-update) | async-done | bytes 12304
  427.5 1.1 copy.16
  428.7 22.7 %psum.15 = f32[4,768]{1,0:T(4,128)S(1)} all-reduce(f32[4,768]{1,0:T(4,128)S(1)} %copy.16), channel_id=1, replica_groups=mesh['pts'=8,'ca'=4,'cb'=4] {'pts'}, use_global_device_ids=true, to_apply=%region_5.6 | all-reduce | flops 3072 | bytes 24576 | tf_op jit(solution)/shard_map/psum | solution.py:52
  (46 shorter events, 12.1 us)
Async XLA Ops:
  7.2 161.6 %all-gather.2.cloned.1.call-start = ((), (), s32[]{:S(2)}) async-start(), calls=%async_computation.1 | async-start | bytes 26738688 | tf_op jit(solution)/shard_map/all_gather | solution.py:32
  7.9 419.6 %reduce-scatter.4.cloned.1.call-start = ((), (), s32[]{:S(2)}) async-start(), calls=%async_computation.2 | async-start | bytes 6684672
Sparse Core Ops, SparseCore 0:
  10.2 158.4 all-gather.1
  347.8 79.6 reduce-scatter.3
where the time goes:
time: 463 us; the launch traced here: 459 us
  waiting for transfers between devices  172 us (37%)
  local copies, waits for them, and re-layouts  109 us (24%)
  blocking collectives  86.2 us (19%)
  other arithmetic  47.1 us (10%)
  matrix products  30.3 us (7%)
  between operations  14.1 us (3%)
    gather x8, local copies, waits for them, and re-layouts, add_block(): jnp.take(cand_blocks, probe_row, axis=0).reshape(PROBES * BLK, feature)  101 us
    all_gather x1, waiting for transfers between devices, local(): gathered = lax.all_gather(candidates, ('ca', 'cb'), axis=0, tiled=True)  91.3 us
    unnamed x3, waiting for transfers between devices  80.5 us
    psum x1, blocking collectives, local(): facility = lax.psum(mine, ('ca', 'cb')).astype(jnp.bfloat16)  63.6 us
    select_n x16, other arithmetic, add_block(): jnp.take(cand_blocks, probe_row, axis=0).reshape(PROBES * BLK, feature)  33.2 us
    dot_general x8, matrix products, add_block(): lax.dot_general(point_rows, taken, dims, preferred_element_type=jnp.float32)  25.2 us
    psum x1, blocking collectives, local(): totals = lax.psum(shares, 'pts')  22.7 us
  transfers between devices with their start and end apart: 2, of which 2 were waited for; matrix products, arithmetic and copies ran while one was open for 1% of the time, Pallas kernels for 0%

commit v1 on v0

v1 whole, which is shorter than its diff:
```python
import functools

import jax
import jax.numpy as jnp
from jax import lax
from jax.experimental import pallas as pl
from jax.experimental.pallas import tpu as pltpu
from jax.sharding import PartitionSpec as P

BLK = 128
PROBES = 24
STEPS = 4
FEATURE = 1024
ROWS = 768
OWN = 1024
QUARTER = 192
PART = 96
HALF = 48
GROUP = 384
SUBS = 12
TILES = 32
FAR = -3e38
NT = (((1,), (1,)), ((), ()))
MESH = pl.DeviceIdType.MESH
A, B = 0, 1

ORDER = (
    (A, 1, 0), (A, 3, 0), (B, 1, 0), (B, 3, 0),
    (A, 0, 3), (A, 0, 1), (B, 0, 3), (B, 0, 1),
    (A, 0, 0), (B, 0, 0), (A, 2, 0), (B, 2, 0),
    (A, 1, 3), (A, 1, 1), (B, 1, 3), (B, 1, 1),
    (A, 3, 3), (A, 3, 1), (B, 3, 3), (B, 3, 1),
    (A, 2, 3), (A, 2, 1), (B, 2, 3), (B, 2, 1),
    (A, 0, 2), (B, 0, 2), (A, 1, 2), (B, 1, 2),
    (A, 3, 2), (B, 3, 2), (A, 2, 2), (B, 2, 2),
)
POS = {key: i for i, key in enumerate(ORDER)}


def tile_of(t):
    group = jnp.where(t < 6, t // 2, jnp.where(t < 9, t - 6, jnp.where(t < 15, 3 + (t - 9) // 3, jnp.where(t < 20, t - 15, 5 + (t - 20) // 4))))
    unit = jnp.where(t < 6, t % 2, jnp.where(t < 9, 2, jnp.where(t < 15, (t - 9) % 3, jnp.where(t < 20, 3, (t - 20) % 4))))
    return group, unit


def kernel(
    points, cands, probes, chosen, gains, cover,
    held, pts, shard, acc, pen, before, bsum, sim0, sim1, lists, fac, sent, got, both, ids,
    loc_sem, cand_s, cand_r, fac_s, fac_r, pt_s, pt_r, aux_s, aux_r, red_s, red_r, last_s, last_r,
):
    me = lax.axis_index("pts")
    y = lax.axis_index("ca")
    z = lax.axis_index("cb")
    x, core = me // 2, me % 2
    quarter = 2 * (x % 2) + core
    way = 1 - 2 * core

    def plane(dy, dz):
        return (me, (y + dy + 4) % 4, (z + dz + 4) % 4)

    sibling = (2 * x + 1 - core, y, z)
    beside = (2 * ((x + way + 4) % 4) + core, y, z)

    def along(part, du, dv):
        return plane(du, dv) if part == A else plane(dv, du)

    def cand_copy(part, du, dv, half=None):
        row, size = POS[part, du, dv] * PART, PART
        if half is not None:
            row, size = row + half * HALF, HALF
        if dv == 0:
            hop_u, hop_v = {1: -1, 3: 1, 2: (1 if half == 0 else -1)}[du], 0
            source = (part, 0, 0) if du != 2 else (part, 3 if half == 0 else 1, 0)
        else:
            hop_u, hop_v = 0, {1: -1, 3: 1, 2: (1 if half == 0 else -1)}[dv]
            source = (part, du, 0) if dv != 2 else (part, du, 3 if half == 0 else 1)
        if source[1:] == (0, 0):
            src = cands.at[pl.ds(quarter * QUARTER + part * PART, PART)]
        else:
            first = POS[source] * PART + (0 if half is None else half * HALF)
            src = held.at[pl.ds(first, size)]
        k = ((part * 4 + du) * 4 + dv) * 2 + (half or 0)
        return pltpu.make_async_remote_copy(
            src_ref=src, dst_ref=held.at[pl.ds(row, size)], send_sem=cand_s.at[k], recv_sem=cand_r.at[k],
            device_id=along(part, hop_u, hop_v), device_id_type=MESH)

    def fac_copy(dy, dz):
        k = ((4 - dy) % 4) * 4 + (4 - dz) % 4
        return pltpu.make_async_remote_copy(
            src_ref=fac.at[0], dst_ref=fac.at[k], send_sem=fac_s.at[k], recv_sem=fac_r.at[k],
            device_id=plane(dy, dz), device_id_type=MESH)

    def remote(src, dst, send, recv, k, device):
        return pltpu.make_async_remote_copy(src_ref=src, dst_ref=dst, send_sem=send.at[k], recv_sem=recv.at[k], device_id=device, device_id_type=MESH)

    def point_copy(kind):
        if kind == 0:
            return remote(points, pts.at[1], pt_s, pt_r, 0, sibling)
        unit = 2 + (kind - 1) % 2
        here = pts.at[unit, pl.ds(core * 512, 512)]
        if kind <= 2:
            return remote(points.at[pl.ds((unit - 2) * 512, 512)], here, pt_s, pt_r, kind, beside)
        return remote(here, here, pt_s, pt_r, kind, sibling)

    def point_landed(kind):
        unit = 2 + (kind - 1) % 2
        there = pts.at[unit, pl.ds((1 - core) * 512, 512)]
        return remote(there, there, pt_s, pt_r, kind, sibling)

    def list_copy(kind):
        if kind == 0:
            return remote(lists.at[0], lists.at[1], aux_s, aux_r, 0, sibling)
        if kind == 1:
            return remote(lists.at[0], lists.at[2 + core], aux_s, aux_r, 1, beside)
        return remote(lists.at[2 + core], lists.at[2 + core], aux_s, aux_r, 2, sibling)

    def before_copy(kind):
        if kind == 0:
            return remote(before.at[0], before.at[1], aux_s, aux_r, 3, sibling)
        unit = 2 + (kind - 1) % 2
        here = before.at[unit, :, pl.ds(core * 512, 512)]
        if kind <= 2:
            return remote(before.at[0, :, pl.ds((unit - 2) * 512, 512)], here, aux_s, aux_r, 3 + kind, beside)
        return remote(here, here, aux_s, aux_r, 3 + kind, sibling)

    def before_landed(kind):
        unit = 2 + (kind - 1) % 2
        there = before.at[unit, :, pl.ds((1 - core) * 512, 512)]
        return remote(there, there, aux_s, aux_r, 3 + kind, sibling)

    def gain_copy(part, du, dv):
        k = part * 16 + ((4 - du) % 4) * 4 + (4 - dv) % 4
        return remote(sent.at[POS[part, du, dv]], got.at[k], red_s, red_r, k, along(part, du, dv))

    def last_copy(k):
        return remote(both.at[me], both.at[me], last_s, last_r, k, ((me + k) % 8, y, z))

    own_points = pltpu.make_async_copy(points, pts.at[0], loc_sem.at[0])
    own_shard = pltpu.make_async_copy(cands, shard, loc_sem.at[1])
    own_parts = pltpu.make_async_copy(cands.at[pl.ds(quarter * QUARTER, QUARTER)], held.at[pl.ds(POS[A, 0, 0] * PART, QUARTER)], loc_sem.at[2])
    own_shard.start()
    own_points.start()
    own_parts.start()
    bar = pltpu.get_barrier_semaphore()
    others = [(dy, dz) for dy in range(4) for dz in range(4) if (dy, dz) != (0, 0)]
    for dy, dz in others:
        pl.semaphore_signal(bar, inc=1, device_id=plane(dy, dz), device_id_type=MESH)
    for k in range(1, 8):
        pl.semaphore_signal(bar, inc=1, device_id=((me + k) % 8, y, z), device_id_type=MESH)

    own_shard.wait()
    row = lax.broadcasted_iota(jnp.int32, (16, ROWS), 0)
    lane = lax.broadcasted_iota(jnp.int32, (16, ROWS), 1)
    pick = jnp.zeros((16, ROWS), jnp.float32)
    for s in range(STEPS):
        local_id = chosen[s] - (y * 4 + z) * ROWS
        pick = jnp.where((row % 4 == s) & (lane == local_id), 1.0, pick)
    mine = jnp.zeros((16, 256), jnp.float32)
    for j in range(4):
        pick_j = jnp.where(row // 4 == j, pick, 0.0).astype(jnp.bfloat16)
        mine = mine + jnp.dot(pick_j, shard[:, j * 256 : (j + 1) * 256], preferred_element_type=jnp.float32)
    fac[0] = mine.astype(jnp.bfloat16)
    lists[0] = jnp.full((8, 128), -1, jnp.int32)
    lists[0, :, 0:PROBES] = probes[...]

    pl.semaphore_wait(bar, 22)
    for dy, dz in others:
        fac_copy(dy, dz).start()
    for key in ((A, 1, 0), (A, 3, 0), (B, 1, 0), (B, 3, 0)):
        cand_copy(*key).start()
    list_copy(0).start()
    list_copy(1).start()
    point_copy(0).start()
    point_copy(1).start()
    for key in ((A, 0, 3), (A, 0, 1), (B, 0, 3), (B, 0, 1)):
        cand_copy(*key).start()

    for i, (part, du, dv) in enumerate(ORDER):
        at_y, at_z = (y + (du, dv)[part]) % 4, (z + (dv, du)[part]) % 4
        for r in range(3):
            ids[i * 3 + r] = (at_y * 4 + at_z) * 6 + (quarter * QUARTER + part * PART + r * 32) // BLK

    def build_pen(unit, listed):
        def one(i, _):
            hit = jnp.max(jnp.where(listed == ids[i], 1.0, 0.0), axis=1, keepdims=True)
            pen[unit, i] = jnp.broadcast_to(jnp.where(hit > 0.0, 0.0, FAR), (8, BLK))
            return 0

        lax.fori_loop(0, 96, one, 0, unroll=8)

    build_pen(0, lists[0])

    def zero(i, _):
        for s in range(STEPS):
            acc[s, pl.ds(i * 384, 384), :] = jnp.zeros((384, BLK), jnp.float32)
        return 0

    lax.fori_loop(0, 9, zero, 0)
    sent[...] = jnp.zeros_like(sent)

    for dy, dz in others:
        fac_copy(dy, dz).wait_recv()
    whole = fac[0].astype(jnp.float32)
    for k in range(1, 16):
        whole = whole + fac[k].astype(jnp.float32)
    wide = jnp.concatenate([whole if j == 0 else pltpu.roll(whole, 16 - 4 * j, 0) for j in range(4)], axis=1).astype(jnp.bfloat16)
    own_points.wait()
    facility_sim = lax.dot_general(wide, pts[0], NT, preferred_element_type=jnp.float32)
    before[0] = jnp.zeros((8, OWN), jnp.float32)
    covered = jnp.zeros((1, OWN), jnp.float32)
    for s in range(STEPS):
        covered = jnp.maximum(covered, facility_sim[s : s + 1, :])
        if s < STEPS - 1:
            before[0, s + 1 : s + 2, :] = covered
    cover[...] = covered
    for kind in (0, 1, 2):
        before_copy(kind).start()
    point_copy(2).start()

    list_copy(0).wait_recv()
    build_pen(1, lists[1])
    point_copy(0).wait_recv()
    before_copy(0).wait_recv()
    own_parts.wait()

    def finalize(group):
        ones = jnp.ones((8, 2 * BLK), jnp.bfloat16)
        for k in range(4):
            for s in range(STEPS):
                total = acc[s, pl.ds(pl.multiple_of(group * GROUP + k * PART, 32), PART), :] - bsum[s : s + 1, :]
                high = total.astype(jnp.bfloat16)
                low = (total - high.astype(jnp.float32)).astype(jnp.bfloat16)
                line = lax.dot_general(ones, jnp.concatenate([high, low], axis=1), NT, preferred_element_type=jnp.float32)
                sent[group * 4 + k, s : s + 1, 0:PART] = line[s : s + 1, :]

    def send_gains(group):
        for part, du, dv in ORDER[group * 4 : group * 4 + 4]:
            if (du, dv) == (0, 0):
                got[part * 16] = sent[POS[part, 0, 0]]
            else:
                gain_copy(part, du, dv).start()

    def at0():
        for key in ((A, 1, 0), (A, 3, 0), (B, 1, 0), (B, 3, 0)):
            cand_copy(*key).wait_recv()
        for part in (A, B):
            for half in (0, 1):
                cand_copy(part, 2, 0, half).start()
        for du in (1, 3):
            for part in (A, B):
                for dv in (3, 1):
                    cand_copy(part, du, dv).start()

    def at2():
        for key in ((A, 0, 3), (A, 0, 1), (B, 0, 3), (B, 0, 1)):
            cand_copy(*key).wait_recv()
        for part in (A, B):
            for half in (0, 1):
                cand_copy(part, 0, 2, half).start()
        list_copy(1).wait_recv()
        list_copy(2).start()
        for kind in (1, 2):
            before_copy(kind).wait_recv()
            before_copy(kind + 2).start()

    def at4():
        for part in (A, B):
            for half in (0, 1):
                cand_copy(part, 2, 0, half).wait_recv()
        for part in (A, B):
            for dv in (3, 1):
                cand_copy(part, 2, dv).start()
        remote(lists.at[3 - core], lists.at[3 - core], aux_s, aux_r, 2, sibling).wait_recv()
        for kind in (3, 4):
            before_landed(kind).wait_recv()
        build_pen(2, jnp.concatenate([lists[2, 0:4], lists[3, 0:4]], axis=0))
        build_pen(3, jnp.concatenate([lists[2, 4:8], lists[3, 4:8]], axis=0))
        total = jnp.zeros((8, BLK), jnp.float32)
        for unit in range(4):
            for j in range(8):
                total = total + before[unit, :, j * BLK : (j + 1) * BLK]
        bsum[...] = total

    def at5():
        point_copy(1).wait_recv()
        point_copy(3).start()

    def at6():
        point_landed(3).wait_recv()

    def s4(du):
        for part in (A, B):
            for dv in (3, 1):
                cand_copy(part, du, dv).wait_recv()
        for part in (A, B):
            for half in (0, 1):
                cand_copy(part, du, 2, half).start()

    def at14():
        point_copy(2).wait_recv()
        point_copy(4).start()

    def at15():
        point_landed(4).wait_recv()

    def halves_landed(*dus):
        for du in dus:
            for part in (A, B):
                for half in (0, 1):
                    cand_copy(part, du, 2, half).wait_recv()

    events = {
        0: at0, 2: at2, 4: at4, 5: at5, 6: at6, 9: lambda: s4(1), 12: lambda: s4(3), 14: at14, 15: at15,
        18: lambda: s4(2), 24: lambda: halves_landed(0, 1), 28: lambda: halves_landed(3, 2),
    }
    done = {17: 0, 18: 1, 19: 2, 20: 3, 21: 4, 25: 5, 29: 6}

    def prepare(t, parity):
        for when, event in events.items():
            if when % 2 == parity:
                pl.when(t == when)(event)
        ready = ((t >= 17) & (t <= 21)) | (t == 25) | (t == 29)
        pl.when(ready)(lambda: finalize(jnp.where(t <= 21, t - 17, jnp.where(t == 25, 5, 6))))
        for when, group in done.items():
            if when % 2 == parity:
                pl.when(t == when)(functools.partial(send_gains, group))

    def product(t, sim):
        group, unit = tile_of(t)
        sim[...] = lax.dot_general(held[pl.ds(pl.multiple_of(group * GROUP, GROUP), GROUP), :], pts[unit], NT, preferred_element_type=jnp.float32)

    def hinge(t, sim):
        group, unit = tile_of(t)
        group = jnp.where(t < 0, 8, group)
        unit = jnp.where(t < 0, 0, unit)
        slot = jnp.where(t < 0, 0, group)
        for r in range(SUBS):
            rows = pl.ds(pl.multiple_of(group * GROUP + r * 32, 32), 32)
            sums = [acc[s, rows, :] for s in range(STEPS)]
            for j in range(8):
                cols = slice(j * BLK, (j + 1) * BLK)
                value = sim[r * 32 : (r + 1) * 32, cols] + pen[unit, slot * SUBS + r, j : j + 1, :]
                sums[0] = sums[0] + jnp.maximum(value, 0.0)
                for s in range(1, STEPS):
                    sums[s] = sums[s] + jnp.maximum(value, before[unit, s : s + 1, cols])
            for s in range(STEPS):
                acc[s, rows, :] = sums[s]

    sim1[...] = jnp.zeros_like(sim1)

    def pair(i, _):
        t = i * 2
        prepare(t, 0)
        product(t, sim0)
        hinge(t - 1, sim1)
        prepare(t + 1, 1)
        product(t + 1, sim1)
        hinge(t, sim0)
        return 0

    lax.fori_loop(0, TILES // 2, pair, 0)
    hinge(jnp.int32(TILES - 1), sim1)
    finalize(jnp.int32(7))
    send_gains(7)

    for part, du, dv in ORDER:
        if (du, dv) != (0, 0):
            gain_copy(part, du, dv).wait_recv()
    for part in (A, B):
        total = got[part * 16]
        for k in range(1, 16):
            total = total + got[part * 16 + k]
        both[me, part] = total
    for k in range(1, 8):
        last_copy(k).start()
    for k in range(1, 8):
        source = both.at[(me + 8 - k) % 8]
        remote(source, source, last_s, last_r, k, ((me + k) % 8, y, z)).wait_recv()
    for q in range(4):
        gains[q] = (both[q] + both[q + 4]) / (BLK * PROBES)

    for part, du, dv in ORDER:
        if (du, dv) != (0, 0):
            gain_copy(part, du, dv).wait_send()
            for half in (0, 1) if 2 in (du, dv) and not (du == 2 and dv in (1, 3)) else (None,):
                cand_copy(part, du, dv, half).wait_send()
    for dy, dz in others:
        fac_copy(dy, dz).wait_send()
    for kind in range(5):
        point_copy(kind).wait_send()
        before_copy(kind).wait_send()
    for kind in range(3):
        list_copy(kind).wait_send()
    for k in range(1, 8):
        last_copy(k).wait_send()


def local(points, candidates, probes, chosen):
    any_spec = pl.BlockSpec(memory_space=pl.ANY)
    vmem = pl.BlockSpec(memory_space=pltpu.VMEM)
    f32, bf16 = jnp.float32, jnp.bfloat16
    dma = pltpu.SemaphoreType.DMA
    gains, cover = pl.pallas_call(
        kernel,
        out_shape=(jax.ShapeDtypeStruct((4, 2, 8, BLK), f32), jax.ShapeDtypeStruct((1, OWN), f32)),
        in_specs=[any_spec, any_spec, vmem, pl.BlockSpec(memory_space=pltpu.SMEM)],
        out_specs=(vmem, vmem),
        scratch_shapes=[
            pltpu.VMEM((32 * PART, FEATURE), bf16),
            pltpu.VMEM((4, OWN, FEATURE), bf16),
            pltpu.VMEM((ROWS, FEATURE), bf16),
            pltpu.VMEM((STEPS, 9 * GROUP, BLK), f32),
            pltpu.VMEM((4, 96, 8, BLK), f32),
            pltpu.VMEM((4, 8, OWN), f32),
            pltpu.VMEM((8, BLK), f32),
            pltpu.VMEM((GROUP, OWN), f32),
            pltpu.VMEM((GROUP, OWN), f32),
            pltpu.VMEM((4, 8, BLK), jnp.int32),
            pltpu.VMEM((16, 16, 256), bf16),
            pltpu.VMEM((32, 8, BLK), f32),
            pltpu.VMEM((32, 8, BLK), f32),
            pltpu.VMEM((8, 2, 8, BLK), f32),
            pltpu.SMEM((96,), jnp.int32),
            dma((3,)),
            dma((64,)), dma((64,)),
            dma((16,)), dma((16,)),
            dma((5,)), dma((5,)),
            dma((8,)), dma((8,)),
            dma((32,)), dma((32,)),
            dma((8,)), dma((8,)),
        ],
        compiler_params=pltpu.CompilerParams(collective_id=0, has_side_effects=True, vmem_limit_bytes=50 << 20),
        name="gather_gain",
    )(points, candidates, probes, chosen)
    gains = gains[:, :, :STEPS, :PART].transpose(2, 0, 1, 3).reshape(STEPS, ROWS)
    return (gains, cover.reshape(OWN))


def solution(mesh):
    return jax.shard_map(
        local,
        mesh=mesh,
        in_specs=(P(("pts", "ca", "cb"), None), P(("ca", "cb"), None), P(("pts", "ca", "cb"), None), P()),
        out_specs=(P(None, ("ca", "cb")), P(("pts", "ca", "cb"))),
        check_vma=False,
    )
```

time: 463 us -> 95.7 us (0.21)
  waiting for transfers between devices: 172 us -> 0 us
  local copies, waits for them, and re-layouts: 109 us -> 5.63 us
  Pallas kernels: 0 us -> 89.2 us
  blocking collectives: 86.2 us -> 0 us
  other arithmetic: 47.1 us -> 0 us
  matrix products: 30.3 us -> 0 us
  between operations: 14.1 us -> 0.67 us
    gather x9 -> x0, local copies, waits for them, and re-layouts: 103 us -> none  [the longest x8 101 us: add_block(): jnp.take(cand_blocks, probe_row, axis=0).reshape(PROBES * BLK, feature)]
    all_gather x1 -> x0, waiting for transfers between devices: 91.3 us -> none  [local(): gathered = lax.all_gather(candidates, ('ca', 'cb'), axis=0, tiled=True)]
    pallas_call x0 -> x1, Pallas kernels: none -> 89.2 us  [local(): pl.pallas_call(kernel, out_shape=(jax.ShapeDtypeStruct((4, 2, 8, BLK), f3...]
    psum x2 -> x0, blocking collectives: 86.2 us -> none  [the longest x1 63.6 us: local(): facility = lax.psum(mine, ('ca', 'cb')).astype(jnp.bfloat16)]
    unnamed x3 -> x0, waiting for transfers between devices: 80.5 us -> none
    select_n x17 -> x0, other arithmetic: 33.2 us -> none  [the longest x16 33.2 us: add_block(): jnp.take(cand_blocks, probe_row, axis=0).reshape(PROBES * BLK, feature)]
    dot_general x17 -> x0, matrix products: 30.3 us -> none  [the longest x8 25.2 us: add_block(): lax.dot_general(point_rows, taken, dims, preferred_element_type=jnp.float32)]
    reduce_sum x8 -> x0, other arithmetic: 6.28 us -> none  [add_block(): summed = jnp.sum(contrib, axis=1).reshape(STEPS, PROBES, BLK)]
  transfers between devices with their start and end apart: 2 -> 0, of which waited for: 2 -> 0; matrix products, arithmetic and copies ran while one was open for 1% -> 0% of each run, Pallas kernels for 0% -> 0%
where the time goes in v1:
time: 95.7 us; the launch traced here: 95.5 us
  Pallas kernels  89.2 us (93%)
  local copies, waits for them, and re-layouts  5.63 us (6%)
    pallas_call x1, Pallas kernels, local(): pl.pallas_call(kernel, out_shape=(jax.ShapeDtypeStruct((4, 2, 8, BLK), f3...  89.2 us
    unnamed x9, local copies, waits for them, and re-layouts  4.93 us

profile of v1, /device:TPU:1, one launch (start us, length us, event | category | flops | bytes accessed | tf_op | source)
XLA Modules:
  0.0 95.5 jit_solution(1849547899345688996)
XLA Ops:
  0.6 0.0 copy-start
  0.6 1.6 %copy-done = bf16[1024,1024]{1,0:T(8,128)(2,1)S(1)} copy-done((bf16[1024,1024]{1,0:T(8,128)(2,1)S(1)}, bf16[1024,1024]{1,0:T(8,128)(2,1)}, u32[]{:S(2)}) %copy-start) | copy-done | bytes 2097176
  2.2 0.0 copy-start.1
  2.2 1.4 %copy-done.1 = bf16[768,1024]{1,0:T(8,128)(2,1)S(1)} copy-done((bf16[768,1024]{1,0:T(8,128)(2,1)S(1)}, bf16[768,1024]{1,0:T(8,128)(2,1)}, u32[]{:S(2)}) %copy-start.1) | copy-done | bytes 1572888
  3.6 0.0 copy-start.2
  3.6 0.7 copy-done.2
  4.3 0.0 copy-start.3
  4.3 0.7 copy-done.3
  5.0 89.2 %gather_gain.1 = (f32[4,2,8,128]{3,2,1,0:T(8,128)S(1)}, f32[1,1024]{1,0:T(1,128)S(1)}) custom-call(bf16[1024,1024]{1,0:T(8,128)(2,1)S(1)} %copy-done, bf16[768,1024]{1,0:T(8,128)(2,1)S(1)} %copy-done.1, s32[8,24]{1,0:T(8,128)S(1)} %copy-done.2, s32[4]{0:T(128)S(1)} %copy-done.3), custom_call_target="tpu_custom_call" | custom-call | tf_op jit(solution)/shard_map/gather_gain/pallas_call | solution.py:403
  94.2 0.7 reshape.10
  94.9 0.6 copy.8
  (2 shorter events, 0.0 us)
Async XLA Ops:
  0.6 1.6 %copy-start = (bf16[1024,1024]{1,0:T(8,128)(2,1)S(1)}, bf16[1024,1024]{1,0:T(8,128)(2,1)}, u32[]{:S(2)}) copy-start(bf16[1024,1024]{1,0:T(8,128)(2,1)} %points.1) | copy-start | bytes 6291460
  2.2 1.4 %copy-start.1 = (bf16[768,1024]{1,0:T(8,128)(2,1)S(1)}, bf16[768,1024]{1,0:T(8,128)(2,1)}, u32[]{:S(2)}) copy-start(bf16[768,1024]{1,0:T(8,128)(2,1)} %cands.1) | copy-start | bytes 4718596
  3.6 0.7 copy-start.2
  4.3 0.7 copy-start.3

commit v2 on v0

v2 whole, which is shorter than its diff:
```python
import functools

import jax
import jax.numpy as jnp
from jax import lax
from jax.experimental import pallas as pl
from jax.experimental.pallas import tpu as pltpu
from jax.sharding import PartitionSpec as P

BLK = 128
PROBES = 24
STEPS = 4
FEATURE = 1024
ROWS = 768
OWN = 1024
QUARTER = 192
PART = 96
HALF = 48
GROUP = 768
UNIT = 512
CHUNK = 256
BLOCKS = 16
NT = (((1,), (1,)), ((), ()))
MESH = pl.DeviceIdType.MESH
A, B = 0, 1


def halves(*keys):
    return [(part, du, dv, h) for part, du, dv in keys for h in (0, 1)]


def ring(du, dvs, hs):
    return [(part, du, dv, h) for part in (A, B) for dv in dvs for h in hs]


FIRST = halves((A, 1, 0), (A, 3, 0), (B, 1, 0), (B, 3, 0))
OPPOSITE = halves((A, 2, 0), (B, 2, 0))
ORDER = (
    halves((A, 0, 0), (B, 0, 0)) + FIRST + ring(0, (3, 1), (0,))
    + ring(0, (3, 1), (1,)) + OPPOSITE + ring(1, (3, 1), (0,)) + ring(1, (3, 1), (1,))
    + ring(3, (3, 1), (0, 1)) + ring(0, (2,), (0, 1)) + ring(2, (3, 1), (0,))
    + ring(2, (3, 1), (1,)) + ring(1, (2,), (0, 1)) + ring(3, (2,), (0, 1)) + ring(2, (2,), (0, 1))
)
POS = {key: i for i, key in enumerate(ORDER)}
WAVES = (
    FIRST, ring(0, (3, 1), (0,)), ring(0, (3, 1), (1,)) + OPPOSITE + ring(1, (3, 1), (0,)), ring(1, (3, 1), (1,)),
    ring(3, (3, 1), (0, 1)) + ring(0, (2,), (0, 1)) + ring(2, (3, 1), (0,)), ring(2, (3, 1), (1,)),
    ring(1, (2,), (0, 1)) + ring(3, (2,), (0, 1)) + ring(2, (2,), (0, 1)),
)
WAVE = {key: i for i, wave in enumerate(WAVES) for key in wave}


def tile_of(t):
    pick = jnp.where
    group = pick(t < 6, 0, pick(t < 12, 1, pick(t < 14, t - 12, pick(t < 22, 2, pick(t < 24, t - 22, 3)))))
    unit = pick(t < 6, t, pick(t < 12, t - 6, pick(t < 14, 6, pick(t < 22, t - 14, pick(t < 24, 7, t - 24)))))
    return group, unit


def kernel(
    points, cands, listed_own, gains, cover,
    held, pts, shard, acc, mask, before, bsum, fsim, sim0, sim1, lists, ids, fac, repeated, sent, got, both,
    loc_sem, cand_s, cand_r, fac_s, fac_r, pt_s, pt_r, aux_s, aux_r, red_s, red_r, last_s, last_r,
):
    me = lax.axis_index("pts")
    y = lax.axis_index("ca")
    z = lax.axis_index("cb")
    x, core = me // 2, me % 2
    quarter = 2 * (x % 2) + core
    way = 1 - 2 * core

    def plane(dy, dz):
        return (me, (y + dy + 4) % 4, (z + dz + 4) % 4)

    sibling = (2 * x + 1 - core, y, z)
    beside = (2 * ((x + way + 4) % 4) + core, y, z)

    def along(part, du, dv):
        return plane(du, dv) if part == A else plane(dv, du)

    def remote(src, dst, send, recv, device, k=0):
        return pltpu.make_async_remote_copy(src_ref=src, dst_ref=dst, send_sem=send.at[0], recv_sem=recv.at[k], device_id=device, device_id_type=MESH)

    def cand_copy(part, du, dv, half):
        row = POS[part, du, dv, half] * HALF
        if dv == 0:
            hop_u, hop_v = {1: -1, 3: 1, 2: (1 if half == 0 else -1)}[du], 0
            source = (part, 0, 0) if du != 2 else (part, 3 if half == 0 else 1, 0)
        else:
            hop_u, hop_v = 0, {1: -1, 3: 1, 2: (1 if half == 0 else -1)}[dv]
            source = (part, du, 0) if dv != 2 else (part, du, 3 if half == 0 else 1)
        if source[1:] == (0, 0):
            src = cands.at[pl.ds(quarter * QUARTER + part * PART + half * HALF, HALF)]
        else:
            src = held.at[pl.ds(POS[source + (half,)] * HALF, HALF)]
        return remote(src, held.at[pl.ds(row, HALF)], cand_s, cand_r, along(part, hop_u, hop_v), WAVE[part, du, dv, half])

    def go(keys):
        for key in keys:
            cand_copy(*key).start()

    def landed(wave):
        at = [i for i, key in enumerate(ORDER) if WAVE.get(key) == wave]
        rows = held.at[pl.ds(at[0] * HALF, len(at) * HALF)]
        remote(rows, rows, cand_s, cand_r, sibling, wave).wait_recv()

    def fac_copy(dy, dz):
        k = ((4 - dy) % 4) * 4 + (4 - dz) % 4
        return remote(fac.at[0], fac.at[k], fac_s, fac_r, plane(dy, dz))

    def own_copy(i):
        return remote(points.at[pl.ds(i * UNIT, UNIT)], pts.at[pl.ds((2 + i) * UNIT, UNIT)], pt_s, pt_r, sibling)

    def chunk_at(i, side):
        return pts.at[pl.ds((4 + i) * UNIT + side * CHUNK, CHUNK)]

    def beside_copy(i):
        return remote(points.at[pl.ds(i * CHUNK, CHUNK)], chunk_at(i, core), pt_s, pt_r, beside, 1 + i)

    def pass_copy(i, side):
        return remote(chunk_at(i, side), chunk_at(i, side), pt_s, pt_r, sibling, 5 + i)

    def list_copy(kind, side):
        if kind == 0:
            return remote(lists.at[0], lists.at[1], aux_s, aux_r, sibling)
        if kind == 1:
            return remote(lists.at[0], lists.at[2 + side], aux_s, aux_r, beside, 1)
        return remote(lists.at[2 + side], lists.at[2 + side], aux_s, aux_r, sibling, 2)

    def gain_copy(part, du, dv):
        k = part * 16 + ((4 - du) % 4) * 4 + (4 - dv) % 4
        return remote(sent.at[(part * 4 + du) * 4 + dv], got.at[k], red_s, red_r, along(part, du, dv))

    def last_copy(k, slot):
        return remote(both.at[slot], both.at[slot], last_s, last_r, ((me + k) % 8, y, z))

    bar = pltpu.get_barrier_semaphore()
    others = [(dy, dz) for dy in range(4) for dz in range(4) if (dy, dz) != (0, 0)]
    for dy, dz in others:
        pl.semaphore_signal(bar, inc=1, device_id=plane(dy, dz), device_id_type=MESH)
    for k in range(1, 8):
        pl.semaphore_signal(bar, inc=1, device_id=((me + k) % 8, y, z), device_id_type=MESH)
    local_copies = [
        pltpu.make_async_copy(cands, shard, loc_sem.at[0]),
        pltpu.make_async_copy(cands.at[pl.ds(quarter * QUARTER, QUARTER)], held.at[pl.ds(0, QUARTER)], loc_sem.at[1]),
        pltpu.make_async_copy(points, pts.at[pl.ds(0, OWN)], loc_sem.at[2]),
    ]
    for copy in local_copies:
        copy.start()
    sent[...] = jnp.zeros_like(sent)
    got[0] = jnp.zeros((8, BLK), jnp.float32)
    got[16] = jnp.zeros((8, BLK), jnp.float32)
    acc[...] = jnp.zeros_like(acc)
    sim1[...] = jnp.zeros_like(sim1)
    lists[0] = listed_own[...]

    local_copies[0].wait()
    row = lax.broadcasted_iota(jnp.int32, (16, ROWS), 0)
    lane = lax.broadcasted_iota(jnp.int32, (16, ROWS), 1)
    pick = jnp.zeros((16, ROWS), jnp.float32)
    for s in range(STEPS):
        wanted = lists[0, :, PROBES + s : PROBES + s + 1] - (y * 4 + z) * ROWS
        pick = jnp.where((row % 4 == s) & (lane == jnp.concatenate([wanted, wanted], axis=0)), 1.0, pick)
    mine = jnp.zeros((16, 256), jnp.float32)
    for j in range(4):
        pick_j = jnp.where(row // 4 == j, pick, 0.0).astype(jnp.bfloat16)
        mine = mine + jnp.dot(pick_j, shard[:, j * 256 : (j + 1) * 256], preferred_element_type=jnp.float32)
    fac[0] = mine.astype(jnp.bfloat16)

    pl.semaphore_wait(bar, 22)
    for dy, dz in others:
        fac_copy(dy, dz).start()
    list_copy(1, core).start()
    list_copy(0, core).start()
    go(key for key in FIRST if key[3] == 0)
    go(key for key in FIRST if key[3] == 1)
    go(ring(0, (3, 1), (0,)))
    go(ring(0, (3, 1), (1,)))
    for i in range(4):
        beside_copy(i).start()
    own_copy(0).start()
    own_copy(1).start()

    lane = lax.broadcasted_iota(jnp.int32, (8, GROUP), 1)
    for g in range(4):
        base = jnp.zeros((8, GROUP), jnp.int32)
        for i, (part, du, dv, h) in enumerate(ORDER[g * 16 : g * 16 + 16]):
            at_y, at_z = (y + (du, dv)[part]) % 4, (z + (dv, du)[part]) % 4
            begin = (at_y * 4 + at_z) * ROWS + quarter * QUARTER + part * PART + (h - i) * HALF
            base = jnp.where(lane >= i * HALF, begin, base)
        ids[g] = lax.shift_right_logical(base + lane, 7)

    def build_mask(unit, listed):
        for g in range(4):
            hit = ids[g] == listed[:, 0:1]
            for k in range(1, PROBES):
                hit = hit | (ids[g] == listed[:, k : k + 1])
            hit = jnp.where(hit, 1.0, 0.0)
            mask[unit, g, 0:4, :] = hit[0:4]
            mask[unit + 1, g, 0:4, :] = hit[4:8]

    build_mask(0, lists[0])
    list_copy(0, core).wait_recv()
    build_mask(2, lists[1])
    list_copy(1, core).wait_recv()
    list_copy(2, core).start()

    slots = fac.at[pl.ds(1, 15)]
    remote(slots, slots, fac_s, fac_r, sibling).wait_recv()
    whole = fac[0].astype(jnp.float32)
    for k in range(1, 16):
        whole = whole + fac[k].astype(jnp.float32)
    wide = jnp.concatenate([whole if j == 0 else pltpu.roll(whole, 16 - 4 * j, 0) for j in range(4)], axis=1).astype(jnp.bfloat16)
    for s in range(3):
        repeated[s * BLK : (s + 1) * BLK, :] = jnp.broadcast_to(wide[s : s + 1, :], (BLK, FEATURE))
    repeated[3 * BLK : 3 * BLK + 16, :] = wide

    def thresholds(unit):
        rows = pl.ds(unit * UNIT, UNIT)
        if not isinstance(unit, int):
            rows = pl.ds(pl.multiple_of(unit * UNIT, UNIT), UNIT)
        fsim[...] = lax.dot_general(pts[rows, :], repeated[0 : 3 * BLK, :], NT, preferred_element_type=jnp.float32)
        for q in range(4):
            sums = [jnp.zeros((8, BLK), jnp.float32) for _ in range(3)]
            for r in range(16):
                at = slice(q * BLK + r * 8, q * BLK + r * 8 + 8)
                covered = jnp.zeros((8, BLK), jnp.float32)
                for s in range(3):
                    covered = jnp.maximum(covered, fsim[at, s * BLK : (s + 1) * BLK])
                    before[unit, s, at, :] = covered
                    sums[s] = sums[s] + covered
            for s in range(3):
                bsum[unit, q, s] = sums[s]

    for copy in local_copies[1:]:
        copy.wait()
    lax.fori_loop(0, 2, lambda u, _: thresholds(u) or 0, 0)
    all_own = pts.at[pl.ds(2 * UNIT, OWN)]
    remote(all_own, all_own, pt_s, pt_r, sibling).wait_recv()
    lax.fori_loop(2, 4, lambda u, _: thresholds(u) or 0, 0)

    list_copy(2, 1 - core).wait_recv()
    left, right = lists[2], lists[3]
    build_mask(4, jnp.concatenate([left[0:2], right[0:2], left[2:4], right[2:4]], axis=0))
    build_mask(6, jnp.concatenate([left[4:6], right[4:6], left[6:8], right[6:8]], axis=0))
    landed(0)

    def send_gains(keys):
        totals = {}
        for part, du, dv in keys:
            pieces = []
            for h in (0, 1):
                g, i = divmod(POS[part, du, dv, h], 16)
                if g not in totals:
                    totals[g] = jnp.sum(acc[g], axis=1)
                pieces.append(totals[g][:, i * HALF : (i + 1) * HALF])
            slot = (part * 4 + du) * 4 + dv
            line = jnp.concatenate(pieces, axis=1)
            if (du, dv) == (0, 0):
                got[part * 16, 0:STEPS, 0:PART] = line
            else:
                sent[slot, 0:STEPS, 0:PART] = line
                gain_copy(part, du, dv).start()

    def coverage():
        facility_sim = lax.dot_general(repeated[3 * BLK : 3 * BLK + 16, :], pts[0:OWN, :], NT, preferred_element_type=jnp.float32)
        covered = jnp.zeros((1, OWN), jnp.float32)
        for s in range(STEPS):
            covered = jnp.maximum(covered, facility_sim[s : s + 1, :])
        cover[...] = covered

    def e0():
        landed(1)
        go(OPPOSITE)
        for du in (1, 3):
            for h in (0, 1):
                go(ring(du, (3, 1), (h,)))
        beside_copy(0).wait_recv()
        pass_copy(0, core).start()

    def e2():
        pass_copy(0, 1 - core).wait_recv()
        thresholds(4)
        beside_copy(1).wait_recv()
        pass_copy(1, core).start()
        coverage()
        pass_copy(1, 1 - core).wait_recv()
        thresholds(5)

    def e3():
        landed(2)
        go(ring(0, (2,), (0, 1)))
        go(ring(2, (3, 1), (0,)))
        go(ring(2, (3, 1), (1,)))
        landed(3)
        go(ring(1, (2,), (0, 1)))

    def e5():
        beside_copy(2).wait_recv()
        pass_copy(2, core).start()

    def e6():
        pass_copy(2, 1 - core).wait_recv()
        thresholds(6)

    def e7():
        landed(4)
        go(ring(3, (2,), (0, 1)))

    def e8():
        landed(5)
        go(ring(2, (2,), (0, 1)))

    def e9():
        beside_copy(3).wait_recv()
        pass_copy(3, core).start()

    def e10():
        pass_copy(3, 1 - core).wait_recv()
        thresholds(7)

    def e12():
        landed(6)
        send_gains([(p, 3, dv) for p in (A, B) for dv in (3, 1)] + [(p, 0, 2) for p in (A, B)])

    def e13():
        send_gains([(p, du, 0) for p in (A, B) for du in (0, 1, 3, 2)] + [(p, du, dv) for p in (A, B) for du in (0, 1) for dv in (3, 1)])

    events = {0: e0, 2: e2, 3: e3, 5: e5, 6: e6, 7: e7, 8: e8, 9: e9, 10: e10, 12: e12, 13: e13}

    def prepare(i, low, high):
        if high - low == 1:
            if low in events:
                events[low]()
            return
        middle = (low + high) // 2
        pl.when(i < middle)(functools.partial(prepare, i, low, middle))
        pl.when(i >= middle)(functools.partial(prepare, i, middle, high))

    def product(t, sim):
        group, unit = tile_of(t)
        sim[...] = lax.dot_general(
            pts[pl.ds(pl.multiple_of(unit * UNIT, UNIT), UNIT), :], held[pl.ds(pl.multiple_of(group * GROUP, GROUP), GROUP), :],
            NT, preferred_element_type=jnp.float32)

    def hinge(t, sim):
        group, unit = tile_of(t)
        unit = jnp.where(t < 0, 0, unit)
        slot = jnp.where(t < 0, 4, group)
        for q in range(4):
            sums = [[None] * 6 for _ in range(STEPS)]
            for r in range(16):
                rows = slice(q * BLK + r * 8, q * BLK + r * 8 + 8)
                floors = [before[unit, s, rows, :] for s in range(3)]
                for c in range(6):
                    value = sim[rows, c * BLK : (c + 1) * BLK]
                    tops = [jnp.maximum(value, 0.0)] + [jnp.maximum(value, floor) for floor in floors]
                    for s in range(STEPS):
                        sums[s][c] = tops[s] if r == 0 else sums[s][c] + tops[s]
            for c in range(6):
                cols = slice(c * BLK, (c + 1) * BLK)
                listed = mask[unit, group, q : q + 1, cols]
                for s in range(STEPS):
                    part = sums[s][c] if s == 0 else sums[s][c] - bsum[unit, q, s - 1]
                    acc[slot, s, :, cols] += part * listed

    def pair(i, _):
        t = i * 2
        prepare(i, 0, BLOCKS)
        product(t, sim0)
        hinge(t - 1, sim1)
        product(t + 1, sim1)
        hinge(t, sim0)
        return 0

    lax.fori_loop(0, BLOCKS, pair, 0)
    hinge(jnp.int32(2 * BLOCKS - 1), sim1)
    send_gains([(p, 2, dv) for p in (A, B) for dv in (3, 1)] + [(p, du, 2) for p in (A, B) for du in (1, 3, 2)])

    arrived = got.at[pl.ds(0, 30)]
    remote(arrived, arrived, red_s, red_r, sibling).wait_recv()
    for part in (A, B):
        total = got[part * 16]
        for k in range(1, 16):
            total = total + got[part * 16 + k]
        both[me, part] = total
    for k in range(1, 8):
        last_copy(k, me).start()
    seven = both.at[pl.ds(0, 7)]
    remote(seven, seven, last_s, last_r, sibling).wait_recv()
    for q in range(4):
        for part in (A, B):
            gains[q, part] = (both[q, part] + both[q + 4, part]) / (BLK * PROBES)

    for ref, send, recv in (
        (held.at[pl.ds(0, 60 * HALF)], cand_s, cand_r),
        (pts.at[pl.ds(0, 3 * OWN)], pt_s, pt_r),
        (slots, fac_s, fac_r),
        (lists.at[pl.ds(0, 3)], aux_s, aux_r),
        (arrived, red_s, red_r),
        (seven, last_s, last_r),
    ):
        remote(ref, ref, send, recv, sibling).wait_send()


def local(points, candidates, probes, chosen):
    hbm, vmem = pl.BlockSpec(memory_space=pltpu.HBM), pl.BlockSpec(memory_space=pltpu.VMEM)
    f32, bf16, i32 = jnp.float32, jnp.bfloat16, jnp.int32
    dma = pltpu.SemaphoreType.DMA
    listed = jnp.pad(probes, ((0, 0), (0, BLK - PROBES))) + jnp.pad(chosen, (PROBES, BLK - PROBES - STEPS))[None, :]
    gains, cover = pl.pallas_call(
        kernel,
        out_shape=(jax.ShapeDtypeStruct((4, 2, 8, BLK), f32), jax.ShapeDtypeStruct((1, OWN), f32)),
        in_specs=[hbm, hbm, vmem],
        out_specs=(vmem, vmem),
        scratch_shapes=[
            pltpu.VMEM((4 * GROUP, FEATURE), bf16),
            pltpu.VMEM((8 * UNIT, FEATURE), bf16),
            pltpu.VMEM((ROWS, FEATURE), bf16),
            pltpu.VMEM((5, STEPS, 8, GROUP), f32),
            pltpu.VMEM((8, 4, 8, GROUP), f32),
            pltpu.VMEM((8, 3, UNIT, BLK), f32),
            pltpu.VMEM((8, 4, 3, 8, BLK), f32),
            pltpu.VMEM((UNIT, 3 * BLK), f32),
            pltpu.VMEM((UNIT, GROUP), f32),
            pltpu.VMEM((UNIT, GROUP), f32),
            pltpu.VMEM((4, 8, BLK), i32),
            pltpu.VMEM((4, 8, GROUP), i32),
            pltpu.VMEM((16, 16, 256), bf16),
            pltpu.VMEM((3 * BLK + 16, FEATURE), bf16),
            pltpu.VMEM((32, 8, BLK), f32),
            pltpu.VMEM((32, 8, BLK), f32),
            pltpu.VMEM((8, 2, 8, BLK), f32),
            dma((3,)),
            dma((1,)), dma((7,)),
            dma((1,)), dma((1,)),
            dma((1,)), dma((9,)),
            dma((1,)), dma((3,)),
            dma((1,)), dma((1,)),
            dma((1,)), dma((1,)),
        ],
        compiler_params=pltpu.CompilerParams(collective_id=0, has_side_effects=True, vmem_limit_bytes=53 << 20),
        name="gather_gain",
    )(points, candidates, listed)
    gains = gains[:, :, :STEPS, :PART].transpose(2, 0, 1, 3).reshape(STEPS, ROWS)
    return (gains, cover.reshape(OWN))


def solution(mesh):
    return jax.shard_map(
        local,
        mesh=mesh,
        in_specs=(P(("pts", "ca", "cb"), None), P(("ca", "cb"), None), P(("pts", "ca", "cb"), None), P()),
        out_specs=(P(None, ("ca", "cb")), P(("pts", "ca", "cb"))),
        check_vma=False,
    )
```

time: 463 us -> 68.4 us (0.15)
  waiting for transfers between devices: 172 us -> 0 us
  local copies, waits for them, and re-layouts: 109 us -> 2.03 us
  blocking collectives: 86.2 us -> 0 us
  Pallas kernels: 0 us -> 64.9 us
  other arithmetic: 47.1 us -> 0.69 us
  matrix products: 30.3 us -> 0 us
  between operations: 14.1 us -> 0.65 us
    gather x9 -> x0, local copies, waits for them, and re-layouts: 103 us -> none  [the longest x8 101 us: add_block(): jnp.take(cand_blocks, probe_row, axis=0).reshape(PROBES * BLK, feature)]
    all_gather x1 -> x0, waiting for transfers between devices: 91.3 us -> none  [local(): gathered = lax.all_gather(candidates, ('ca', 'cb'), axis=0, tiled=True)]
    psum x2 -> x0, blocking collectives: 86.2 us -> none  [the longest x1 63.6 us: local(): facility = lax.psum(mine, ('ca', 'cb')).astype(jnp.bfloat16)]
    unnamed x3 -> x0, waiting for transfers between devices: 80.5 us -> none
    pallas_call x0 -> x1, Pallas kernels: none -> 64.9 us  [local(): pl.pallas_call(kernel, out_shape=(jax.ShapeDtypeStruct((4, 2, 8, BLK), f3...]
    select_n x17 -> x0, other arithmetic: 33.2 us -> none  [the longest x16 33.2 us: add_block(): jnp.take(cand_blocks, probe_row, axis=0).reshape(PROBES * BLK, feature)]
    dot_general x17 -> x0, matrix products: 30.3 us -> none  [the longest x8 25.2 us: add_block(): lax.dot_general(point_rows, taken, dims, preferred_element_type=jnp.float32)]
    reduce_sum x8 -> x0, other arithmetic: 6.28 us -> none  [add_block(): summed = jnp.sum(contrib, axis=1).reshape(STEPS, PROBES, BLK)]
  transfers between devices with their start and end apart: 2 -> 0, of which waited for: 2 -> 0; matrix products, arithmetic and copies ran while one was open for 1% -> 0% of each run, Pallas kernels for 0% -> 0%
where the time goes in v2:
time: 68.4 us; the launch traced here: 68.2 us
  Pallas kernels  64.9 us (95%)
  local copies, waits for them, and re-layouts  2.03 us (3%)
  other arithmetic  0.69 us (1%)
    pallas_call x1, Pallas kernels, local(): pl.pallas_call(kernel, out_shape=(jax.ShapeDtypeStruct((4, 2, 8, BLK), f3...  64.9 us

profile of v2, /device:TPU:1, one launch (start us, length us, event | category | flops | bytes accessed | tf_op | source)
XLA Modules:
  0.0 68.2 jit_solution(6999621999248007545)
XLA Ops:
  0.6 0.7 %pad.9 = s32[128]{0:T(128)S(1)} pad(s32[4]{0:T(128)} %param.7, s32[]{:T(128)} %constant.0.clone.1), padding=24_100 | pad | bytes 532 | tf_op jit(solution)/shard_map/jit(_pad)/pad | solution.py:410
  1.4 0.7 %pad_add_fusion.listed_own = s32[8,128]{1,0:T(8,128)S(1)} fusion(s32[8,24]{1,0:T(8,128)} %param.6, s32[128]{0:T(128)S(1)} %pad.9), kind=kLoop, calls=%fused_computation.1 | loop fusion | flops 1024 | bytes 5376 | tf_op jit(solution)/shard_map/add | solution.py:410
  2.1 64.9 %gather_gain.1 = (f32[4,2,8,128]{3,2,1,0:T(8,128)S(1)}, f32[1,1024]{1,0:T(1,128)S(1)}) custom-call(bf16[1024,1024]{1,0:T(8,128)(2,1)} %points.1, bf16[768,1024]{1,0:T(8,128)(2,1)} %cands.1, s32[8,128]{1,0:T(8,128)S(1)} %pad_add_fusion.listed_own), custom_call_target="tpu_custom_call" | custom-call | tf_op jit(solution)/shard_map/gather_gain/pallas_call | solution.py:411
  66.9 0.7 %reshape.11 = f32[4,768]{1,0:T(4,128)} reshape(f32[4,4,2,96]{3,2,1,0:T(2,128)S(1)} %copy.6) | data formatting | bytes 24576 | tf_op jit(solution)/shard_map/reshape | solution.py:445
  67.6 0.6 copy.8
  (2 shorter events, 0.0 us)

commit v3 on v2

--- a/solution.py
+++ b/solution.py
@@ -37,14 +37,14 @@
 OPPOSITE = halves((A, 2, 0), (B, 2, 0))
 ORDER = (
     halves((A, 0, 0), (B, 0, 0)) + FIRST + ring(0, (3, 1), (0,))
-    + ring(0, (3, 1), (1,)) + OPPOSITE + ring(1, (3, 1), (0,)) + ring(1, (3, 1), (1,))
+    + ring(0, (3, 1), (1,)) + OPPOSITE + ring(1, (3, 1), (0, 1))
     + ring(3, (3, 1), (0, 1)) + ring(0, (2,), (0, 1)) + ring(2, (3, 1), (0,))
     + ring(2, (3, 1), (1,)) + ring(1, (2,), (0, 1)) + ring(3, (2,), (0, 1)) + ring(2, (2,), (0, 1))
 )
 POS = {key: i for i, key in enumerate(ORDER)}
 WAVES = (
-    FIRST, ring(0, (3, 1), (0,)), ring(0, (3, 1), (1,)) + OPPOSITE + ring(1, (3, 1), (0,)), ring(1, (3, 1), (1,)),
-    ring(3, (3, 1), (0, 1)) + ring(0, (2,), (0, 1)) + ring(2, (3, 1), (0,)), ring(2, (3, 1), (1,)),
+    FIRST, ring(0, (3, 1), (0,)), ring(0, (3, 1), (1,)) + OPPOSITE, ring(1, (3, 1), (0, 1)),
+    ring(3, (3, 1), (0, 1)), ring(0, (2,), (0, 1)) + ring(2, (3, 1), (0,)), ring(2, (3, 1), (1,)),
     ring(1, (2,), (0, 1)) + ring(3, (2,), (0, 1)) + ring(2, (2,), (0, 1)),
 )
 WAVE = {key: i for i, wave in enumerate(WAVES) for key in wave}
@@ -59,8 +59,8 @@
 
 def kernel(
     points, cands, listed_own, gains, cover,
-    held, pts, shard, acc, mask, before, bsum, fsim, sim0, sim1, lists, ids, fac, repeated, sent, got, both,
-    loc_sem, cand_s, cand_r, fac_s, fac_r, pt_s, pt_r, aux_s, aux_r, red_s, red_r, last_s, last_r,
+    held, pts, shard, acc, mask, before, fsim, sim0, sim1, lists, ids, fac, columns, repeated, sent, got, both,
+    loc_sem, cand_s, cand_r, fac_s, fac_r, col_s, col_r, pt_s, pt_r, aux_s, aux_r, thr_s, thr_r, red_s, red_r, last_s, last_r,
 ):
     me = lax.axis_index("pts")
     y = lax.axis_index("ca")
@@ -108,6 +108,9 @@
         k = ((4 - dy) % 4) * 4 + (4 - dz) % 4
         return remote(fac.at[0], fac.at[k], fac_s, fac_r, plane(dy, dz))
 
+    def column_copy(side):
+        return remote(columns.at[side], columns.at[side], col_s, col_r, sibling)
+
     def own_copy(i):
         return remote(points.at[pl.ds(i * UNIT, UNIT)], pts.at[pl.ds((2 + i) * UNIT, UNIT)], pt_s, pt_r, sibling)
 
@@ -126,6 +129,13 @@
         if kind == 1:
             return remote(lists.at[0], lists.at[2 + side], aux_s, aux_r, beside, 1)
         return remote(lists.at[2 + side], lists.at[2 + side], aux_s, aux_r, sibling, 2)
+
+    def own_before_copy(unit):
+        return remote(before.at[unit], before.at[2 + unit], thr_s, thr_r, sibling)
+
+    def before_copy(i, side):
+        here = before.at[4 + i, :, side]
+        return remote(here, here, thr_s, thr_r, sibling, 1 + i)
 
     def gain_copy(part, du, dv):
         k = part * 16 + ((4 - du) % 4) * 4 + (4 - dv) % 4
@@ -141,12 +151,11 @@
     for k in range(1, 8):
         pl.semaphore_signal(bar, inc=1, device_id=((me + k) % 8, y, z), device_id_type=MESH)
     local_copies = [
-        pltpu.make_async_copy(cands, shard, loc_sem.at[0]),
+        pltpu.make_async_copy(cands.at[:, pl.ds(pl.multiple_of(core * 512, 512), 512)], shard, loc_sem.at[0]),
         pltpu.make_async_copy(cands.at[pl.ds(quarter * QUARTER, QUARTER)], held.at[pl.ds(0, QUARTER)], loc_sem.at[1]),
         pltpu.make_async_copy(points, pts.at[pl.ds(0, OWN)], loc_sem.at[2]),
     ]
-    for copy in local_copies:
-        copy.start()
+    local_copies[0].start()
     sent[...] = jnp.zeros_like(sent)
     got[0] = jnp.zeros((8, BLK), jnp.float32)
     got[16] = jnp.zeros((8, BLK), jnp.float32)
@@ -155,16 +164,18 @@
     lists[0] = listed_own[...]
 
     local_copies[0].wait()
+    for copy in local_copies[1:]:
+        copy.start()
     row = lax.broadcasted_iota(jnp.int32, (16, ROWS), 0)
     lane = lax.broadcasted_iota(jnp.int32, (16, ROWS), 1)
     pick = jnp.zeros((16, ROWS), jnp.float32)
     for s in range(STEPS):
         wanted = lists[0, :, PROBES + s : PROBES + s + 1] - (y * 4 + z) * ROWS
         pick = jnp.where((row % 4 == s) & (lane == jnp.concatenate([wanted, wanted], axis=0)), 1.0, pick)
-    mine = jnp.zeros((16, 256), jnp.float32)
+    mine = jnp.zeros((16, BLK), jnp.float32)
     for j in range(4):
         pick_j = jnp.where(row // 4 == j, pick, 0.0).astype(jnp.bfloat16)
-        mine = mine + jnp.dot(pick_j, shard[:, j * 256 : (j + 1) * 256], preferred_element_type=jnp.float32)
+        mine = mine + jnp.dot(pick_j, shard[:, j * BLK : (j + 1) * BLK], preferred_element_type=jnp.float32)
     fac[0] = mine.astype(jnp.bfloat16)
 
     pl.semaphore_wait(bar, 22)
@@ -176,7 +187,7 @@
     go(key for key in FIRST if key[3] == 1)
     go(ring(0, (3, 1), (0,)))
     go(ring(0, (3, 1), (1,)))
-    for i in range(4):
+    for i in range(2):
         beside_copy(i).start()
     own_copy(0).start()
     own_copy(1).start()
@@ -202,48 +213,71 @@
     build_mask(0, lists[0])
     list_copy(0, core).wait_recv()
     build_mask(2, lists[1])
-    list_copy(1, core).wait_recv()
-    list_copy(2, core).start()
 
     slots = fac.at[pl.ds(1, 15)]
     remote(slots, slots, fac_s, fac_r, sibling).wait_recv()
     whole = fac[0].astype(jnp.float32)
     for k in range(1, 16):
         whole = whole + fac[k].astype(jnp.float32)
-    wide = jnp.concatenate([whole if j == 0 else pltpu.roll(whole, 16 - 4 * j, 0) for j in range(4)], axis=1).astype(jnp.bfloat16)
+    columns[core] = whole.astype(jnp.bfloat16)
+    column_copy(core).start()
+    list_copy(1, core).wait_recv()
+    list_copy(2, core).start()
+    column_copy(1 - core).wait_recv()
+    pieces = [columns[side].astype(jnp.float32) for side in (0, 1)]
+    wide = jnp.concatenate([piece if j == 0 else pltpu.roll(piece, 16 - 4 * j, 0) for piece in pieces for j in range(4)], axis=1).astype(jnp.bfloat16)
     for s in range(3):
         repeated[s * BLK : (s + 1) * BLK, :] = jnp.broadcast_to(wide[s : s + 1, :], (BLK, FEATURE))
-    repeated[3 * BLK : 3 * BLK + 16, :] = wide
-
-    def thresholds(unit):
-        rows = pl.ds(unit * UNIT, UNIT)
-        if not isinstance(unit, int):
-            rows = pl.ds(pl.multiple_of(unit * UNIT, UNIT), UNIT)
-        fsim[...] = lax.dot_general(pts[rows, :], repeated[0 : 3 * BLK, :], NT, preferred_element_type=jnp.float32)
-        for q in range(4):
-            sums = [jnp.zeros((8, BLK), jnp.float32) for _ in range(3)]
-            for r in range(16):
-                at = slice(q * BLK + r * 8, q * BLK + r * 8 + 8)
-                covered = jnp.zeros((8, BLK), jnp.float32)
+
+    def thresholds(row, unit, sides):
+        count = len(sides) * CHUNK
+        fsim[0:count] = lax.dot_general(pts[pl.ds(row, count), :], repeated[...], NT, preferred_element_type=jnp.float32)
+        for i, side in enumerate(sides):
+            for q in range(2):
+                sums = [jnp.zeros((8, BLK), jnp.float32) for _ in range(3)]
+                for r in range(16):
+                    at = i * CHUNK + q * BLK + r * 8
+                    covered = jnp.zeros((8, BLK), jnp.float32)
+                    for s in range(3):
+                        covered = jnp.maximum(covered, fsim[at : at + 8, s * BLK : (s + 1) * BLK])
+                        before[unit, s, side, q * BLK + r * 8 : q * BLK + r * 8 + 8, :] = covered
+                        sums[s] = sums[s] + covered
                 for s in range(3):
-                    covered = jnp.maximum(covered, fsim[at, s * BLK : (s + 1) * BLK])
-                    before[unit, s, at, :] = covered
-                    sums[s] = sums[s] + covered
-            for s in range(3):
-                bsum[unit, q, s] = sums[s]
+                    before[unit, s, side, CHUNK + q * 8 : CHUNK + q * 8 + 8, :] = sums[s]
+
+    def beside_landed(i):
+        beside_copy(i).wait_recv()
+        pass_copy(i, core).start()
+        thresholds(pl.multiple_of((4 + i) * UNIT + core * CHUNK, CHUNK), 4 + i, (core,))
+        before_copy(i, core).start()
+
+    def passed_landed(i):
+        pass_copy(i, 1 - core).wait_recv()
+        before_copy(i, 1 - core).wait_recv()
 
     for copy in local_copies[1:]:
         copy.wait()
-    lax.fori_loop(0, 2, lambda u, _: thresholds(u) or 0, 0)
+    for unit in (0, 1):
+        thresholds(unit * UNIT, unit, (0, 1))
+        own_before_copy(unit).start()
+    landed(0)
+    go(OPPOSITE)
+    for du in (1, 3):
+        for h in (0, 1):
+            go(ring(du, (3, 1), (h,)))
     all_own = pts.at[pl.ds(2 * UNIT, OWN)]
     remote(all_own, all_own, pt_s, pt_r, sibling).wait_recv()
-    lax.fori_loop(2, 4, lambda u, _: thresholds(u) or 0, 0)
 
     list_copy(2, 1 - core).wait_recv()
     left, right = lists[2], lists[3]
     build_mask(4, jnp.concatenate([left[0:2], right[0:2], left[2:4], right[2:4]], axis=0))
     build_mask(6, jnp.concatenate([left[4:6], right[4:6], left[6:8], right[6:8]], axis=0))
-    landed(0)
+
+    facility_sim = lax.dot_general(wide, pts[0:OWN, :], NT, preferred_element_type=jnp.float32)
+    covered = jnp.zeros((1, OWN), jnp.float32)
+    for s in range(STEPS):
+        covered = jnp.maximum(covered, facility_sim[s : s + 1, :])
+    cover[...] = covered
 
     def send_gains(keys):
         totals = {}
@@ -262,71 +296,58 @@
                 sent[slot, 0:STEPS, 0:PART] = line
                 gain_copy(part, du, dv).start()
 
-    def coverage():
-        facility_sim = lax.dot_general(repeated[3 * BLK : 3 * BLK + 16, :], pts[0:OWN, :], NT, preferred_element_type=jnp.float32)
-        covered = jnp.zeros((1, OWN), jnp.float32)
-        for s in range(STEPS):
-            covered = jnp.maximum(covered, facility_sim[s : s + 1, :])
-        cover[...] = covered
-
     def e0():
         landed(1)
-        go(OPPOSITE)
-        for du in (1, 3):
-            for h in (0, 1):
-                go(ring(du, (3, 1), (h,)))
-        beside_copy(0).wait_recv()
-        pass_copy(0, core).start()
+
+    def e1():
+        beside_copy(2).start()
+        beside_landed(0)
+        theirs = before.at[pl.ds(2, 2)]
+        remote(theirs, theirs, thr_s, thr_r, sibling).wait_recv()
 
     def e2():
-        pass_copy(0, 1 - core).wait_recv()
-        thresholds(4)
-        beside_copy(1).wait_recv()
-        pass_copy(1, core).start()
-        coverage()
-        pass_copy(1, 1 - core).wait_recv()
-        thresholds(5)
-
-    def e3():
+        beside_landed(1)
         landed(2)
         go(ring(0, (2,), (0, 1)))
         go(ring(2, (3, 1), (0,)))
         go(ring(2, (3, 1), (1,)))
+        passed_landed(0)
+        passed_landed(1)
+
+    def e3():
+        beside_copy(3).start()
         landed(3)
         go(ring(1, (2,), (0, 1)))
 
     def e5():
-        beside_copy(2).wait_recv()
-        pass_copy(2, core).start()
-
-    def e6():
-        pass_copy(2, 1 - core).wait_recv()
-        thresholds(6)
-
-    def e7():
         landed(4)
         go(ring(3, (2,), (0, 1)))
+        beside_landed(2)
+
+    def e6():
+        passed_landed(2)
+
+    def e7():
+        landed(5)
 
     def e8():
-        landed(5)
+        landed(6)
         go(ring(2, (2,), (0, 1)))
 
     def e9():
-        beside_copy(3).wait_recv()
-        pass_copy(3, core).start()
+        beside_landed(3)
 
     def e10():
-        pass_copy(3, 1 - core).wait_recv()
-        thresholds(7)
+        passed_landed(3)
 
     def e12():
-        landed(6)
+        landed(7)
         send_gains([(p, 3, dv) for p in (A, B) for dv in (3, 1)] + [(p, 0, 2) for p in (A, B)])
 
     def e13():
         send_gains([(p, du, 0) for p in (A, B) for du in (0, 1, 3, 2)] + [(p, du, dv) for p in (A, B) for du in (0, 1) for dv in (3, 1)])
 
-    events = {0: e0, 2: e2, 3: e3, 5: e5, 6: e6, 7: e7, 8: e8, 9: e9, 10: e10, 12: e12, 13: e13}
+    events = {0: e0, 1: e1, 2: e2, 3: e3, 5: e5, 6: e6, 7: e7, 8: e8, 9: e9, 10: e10, 12: e12, 13: e13}
 
     def prepare(i, low, high):
         if high - low == 1:
@@ -351,7 +372,7 @@
             sums = [[None] * 6 for _ in range(STEPS)]
             for r in range(16):
                 rows = slice(q * BLK + r * 8, q * BLK + r * 8 + 8)
-                floors = [before[unit, s, rows, :] for s in range(3)]
+                floors = [before[unit, s, q // 2, q % 2 * BLK + r * 8 : q % 2 * BLK + r * 8 + 8, :] for s in range(3)]
                 for c in range(6):
                     value = sim[rows, c * BLK : (c + 1) * BLK]
                     tops = [jnp.maximum(value, 0.0)] + [jnp.maximum(value, floor) for floor in floors]
@@ -361,7 +382,7 @@
                 cols = slice(c * BLK, (c + 1) * BLK)
                 listed = mask[unit, group, q : q + 1, cols]
                 for s in range(STEPS):
-                    part = sums[s][c] if s == 0 else sums[s][c] - bsum[unit, q, s - 1]
+                    part = sums[s][c] if s == 0 else sums[s][c] - before[unit, s - 1, q // 2, CHUNK + q % 2 * 8 : CHUNK + q % 2 * 8 + 8, :]
                     acc[slot, s, :, cols] += part * listed
 
     def pair(i, _):
@@ -396,7 +417,9 @@
         (held.at[pl.ds(0, 60 * HALF)], cand_s, cand_r),
         (pts.at[pl.ds(0, 3 * OWN)], pt_s, pt_r),
         (slots, fac_s, fac_r),
+        (columns.at[0], col_s, col_r),
         (lists.at[pl.ds(0, 3)], aux_s, aux_r),
+        (before.at[pl.ds(0, 4)], thr_s, thr_r),
         (arrived, red_s, red_r),
         (seven, last_s, last_r),
     ):
@@ -416,26 +439,28 @@
         scratch_shapes=[
             pltpu.VMEM((4 * GROUP, FEATURE), bf16),
             pltpu.VMEM((8 * UNIT, FEATURE), bf16),
-            pltpu.VMEM((ROWS, FEATURE), bf16),
+            pltpu.VMEM((ROWS, FEATURE // 2), bf16),
             pltpu.VMEM((5, STEPS, 8, GROUP), f32),
             pltpu.VMEM((8, 4, 8, GROUP), f32),
-            pltpu.VMEM((8, 3, UNIT, BLK), f32),
-            pltpu.VMEM((8, 4, 3, 8, BLK), f32),
+            pltpu.VMEM((8, 3, 2, CHUNK + 16, BLK), f32),
             pltpu.VMEM((UNIT, 3 * BLK), f32),
             pltpu.VMEM((UNIT, GROUP), f32),
             pltpu.VMEM((UNIT, GROUP), f32),
             pltpu.VMEM((4, 8, BLK), i32),
             pltpu.VMEM((4, 8, GROUP), i32),
-            pltpu.VMEM((16, 16, 256), bf16),
-            pltpu.VMEM((3 * BLK + 16, FEATURE), bf16),
+            pltpu.VMEM((16, 16, BLK), bf16),
+            pltpu.VMEM((2, 16, BLK), bf16),
+            pltpu.VMEM((3 * BLK, FEATURE), bf16),
             pltpu.VMEM((32, 8, BLK), f32),
             pltpu.VMEM((32, 8, BLK), f32),
             pltpu.VMEM((8, 2, 8, BLK), f32),
             dma((3,)),
-            dma((1,)), dma((7,)),
+            dma((1,)), dma((8,)),
+            dma((1,)), dma((1,)),
             dma((1,)), dma((1,)),
             dma((1,)), dma((9,)),
             dma((1,)), dma((3,)),
+            dma((1,)), dma((5,)),
             dma((1,)), dma((1,)),
             dma((1,)), dma((1,)),
         ],

time: 68.4 us -> 66.7 us (0.975)
  Pallas kernels: 64.9 us -> 63.1 us
    pallas_call x1, Pallas kernels: 64.9 us -> 63.1 us  [local(): pl.pallas_call(kernel, out_shape=(jax.ShapeDtypeStruct((4, 2, 8, BLK), f3...]
where the time goes in v3:
time: 66.7 us; the launch traced here: 66.5 us
  Pallas kernels  63.1 us (95%)
  local copies, waits for them, and re-layouts  2.03 us (3%)
  other arithmetic  0.69 us (1%)
    pallas_call x1, Pallas kernels, local(): pl.pallas_call(kernel, out_shape=(jax.ShapeDtypeStruct((4, 2, 8, BLK), f3...  63.1 us

profile of v3, /device:TPU:1, one launch (start us, length us, event | category | flops | bytes accessed | tf_op | source)
XLA Modules:
  0.0 66.5 jit_solution(357863857856906664)
XLA Ops:
  0.6 0.7 %pad.9 = s32[128]{0:T(128)S(1)} pad(s32[4]{0:T(128)} %param.7, s32[]{:T(128)} %constant.0.clone.1), padding=24_100 | pad | bytes 532 | tf_op jit(solution)/shard_map/jit(_pad)/pad | solution.py:433
  1.4 0.7 %pad_add_fusion.listed_own = s32[8,128]{1,0:T(8,128)S(1)} fusion(s32[8,24]{1,0:T(8,128)} %param.6, s32[128]{0:T(128)S(1)} %pad.9), kind=kLoop, calls=%fused_computation.1 | loop fusion | flops 1024 | bytes 5376 | tf_op jit(solution)/shard_map/add | solution.py:433
  2.1 63.1 %gather_gain.1 = (f32[4,2,8,128]{3,2,1,0:T(8,128)S(1)}, f32[1,1024]{1,0:T(1,128)S(1)}) custom-call(bf16[1024,1024]{1,0:T(8,128)(2,1)} %points.1, bf16[768,1024]{1,0:T(8,128)(2,1)} %cands.1, s32[8,128]{1,0:T(8,128)S(1)} %pad_add_fusion.listed_own), custom_call_target="tpu_custom_call" | custom-call | tf_op jit(solution)/shard_map/gather_gain/pallas_call | solution.py:434
  65.2 0.7 %reshape.11 = f32[4,768]{1,0:T(4,128)} reshape(f32[4,4,2,96]{3,2,1,0:T(2,128)S(1)} %copy.6) | data formatting | bytes 24576 | tf_op jit(solution)/shard_map/reshape | solution.py:470
  65.9 0.6 copy.8
  (2 shorter events, 0.0 us)

commit v4 on v3

--- a/solution.py
+++ b/solution.py
@@ -312,10 +312,11 @@
         go(ring(2, (3, 1), (0,)))
         go(ring(2, (3, 1), (1,)))
         passed_landed(0)
-        passed_landed(1)
+        pass_copy(1, 1 - core).wait_recv()
 
     def e3():
         beside_copy(3).start()
+        before_copy(1, 1 - core).wait_recv()
         landed(3)
         go(ring(1, (2,), (0, 1)))
 
@@ -338,7 +339,10 @@
         beside_landed(3)
 
     def e10():
-        passed_landed(3)
+        pass_copy(3, 1 - core).wait_recv()
+
+    def e11():
+        before_copy(3, 1 - core).wait_recv()
 
     def e12():
         landed(7)
@@ -347,7 +351,7 @@
     def e13():
         send_gains([(p, du, 0) for p in (A, B) for du in (0, 1, 3, 2)] + [(p, du, dv) for p in (A, B) for du in (0, 1) for dv in (3, 1)])
 
-    events = {0: e0, 1: e1, 2: e2, 3: e3, 5: e5, 6: e6, 7: e7, 8: e8, 9: e9, 10: e10, 12: e12, 13: e13}
+    events = {0: e0, 1: e1, 2: e2, 3: e3, 5: e5, 6: e6, 7: e7, 8: e8, 9: e9, 10: e10, 11: e11, 12: e12, 13: e13}
 
     def prepare(i, low, high):
         if high - low == 1:

time: 66.7 us -> 66.7 us (level)
  no operation moved by 1% of the time
where the time goes in v4:
time: 66.7 us; the launch traced here: 66.5 us
  Pallas kernels  63.1 us (95%)
  local copies, waits for them, and re-layouts  2.03 us (3%)
  other arithmetic  0.69 us (1%)
    pallas_call x1, Pallas kernels, local(): pl.pallas_call(kernel, out_shape=(jax.ShapeDtypeStruct((4, 2, 8, BLK), f3...  63.1 us

profile of v4, /device:TPU:1, one launch (start us, length us, event | category | flops | bytes accessed | tf_op | source)
XLA Modules:
  0.0 66.5 jit_solution(17775223008240877973)
XLA Ops:
  0.6 0.7 %pad.9 = s32[128]{0:T(128)S(1)} pad(s32[4]{0:T(128)} %param.7, s32[]{:T(128)} %constant.0.clone.1), padding=24_100 | pad | bytes 532 | tf_op jit(solution)/shard_map/jit(_pad)/pad | solution.py:437
  1.4 0.7 %pad_add_fusion.listed_own = s32[8,128]{1,0:T(8,128)S(1)} fusion(s32[8,24]{1,0:T(8,128)} %param.6, s32[128]{0:T(128)S(1)} %pad.9), kind=kLoop, calls=%fused_computation.1 | loop fusion | flops 1024 | bytes 5376 | tf_op jit(solution)/shard_map/add | solution.py:437
  2.1 63.1 %gather_gain.1 = (f32[4,2,8,128]{3,2,1,0:T(8,128)S(1)}, f32[1,1024]{1,0:T(1,128)S(1)}) custom-call(bf16[1024,1024]{1,0:T(8,128)(2,1)} %points.1, bf16[768,1024]{1,0:T(8,128)(2,1)} %cands.1, s32[8,128]{1,0:T(8,128)S(1)} %pad_add_fusion.listed_own), custom_call_target="tpu_custom_call" | custom-call | tf_op jit(solution)/shard_map/gather_gain/pallas_call | solution.py:438
  65.2 0.7 %reshape.11 = f32[4,768]{1,0:T(4,128)} reshape(f32[4,4,2,96]{3,2,1,0:T(2,128)S(1)} %copy.6) | data formatting | bytes 24576 | tf_op jit(solution)/shard_map/reshape | solution.py:474
  65.9 0.6 copy.8
  (2 shorter events, 0.0 us)

commit v5 on v4

--- a/solution.py
+++ b/solution.py
@@ -179,16 +179,16 @@
     fac[0] = mine.astype(jnp.bfloat16)
 
     pl.semaphore_wait(bar, 22)
+    list_copy(1, core).start()
+    list_copy(0, core).start()
+    for i in range(2):
+        beside_copy(i).start()
     for dy, dz in others:
         fac_copy(dy, dz).start()
-    list_copy(1, core).start()
-    list_copy(0, core).start()
     go(key for key in FIRST if key[3] == 0)
     go(key for key in FIRST if key[3] == 1)
     go(ring(0, (3, 1), (0,)))
     go(ring(0, (3, 1), (1,)))
-    for i in range(2):
-        beside_copy(i).start()
     own_copy(0).start()
     own_copy(1).start()
 

time: 66.7 us -> 66.7 us (level)
  no operation moved by 1% of the time
where the time goes in v5:
time: 66.7 us; the launch traced here: 66.5 us
  Pallas kernels  63.1 us (95%)
  local copies, waits for them, and re-layouts  2.03 us (3%)
  other arithmetic  0.69 us (1%)
    pallas_call x1, Pallas kernels, local(): pl.pallas_call(kernel, out_shape=(jax.ShapeDtypeStruct((4, 2, 8, BLK), f3...  63.1 us

profile of v5, /device:TPU:1, one launch (start us, length us, event | category | flops | bytes accessed | tf_op | source)
XLA Modules:
  0.0 66.5 jit_solution(7728565824018061807)
XLA Ops:
  0.6 0.7 %pad.9 = s32[128]{0:T(128)S(1)} pad(s32[4]{0:T(128)} %param.7, s32[]{:T(128)} %constant.0.clone.1), padding=24_100 | pad | bytes 532 | tf_op jit(solution)/shard_map/jit(_pad)/pad | solution.py:437
  1.4 0.7 %pad_add_fusion.listed_own = s32[8,128]{1,0:T(8,128)S(1)} fusion(s32[8,24]{1,0:T(8,128)} %param.6, s32[128]{0:T(128)S(1)} %pad.9), kind=kLoop, calls=%fused_computation.1 | loop fusion | flops 1024 | bytes 5376 | tf_op jit(solution)/shard_map/add | solution.py:437
  2.1 63.1 %gather_gain.1 = (f32[4,2,8,128]{3,2,1,0:T(8,128)S(1)}, f32[1,1024]{1,0:T(1,128)S(1)}) custom-call(bf16[1024,1024]{1,0:T(8,128)(2,1)} %points.1, bf16[768,1024]{1,0:T(8,128)(2,1)} %cands.1, s32[8,128]{1,0:T(8,128)S(1)} %pad_add_fusion.listed_own), custom_call_target="tpu_custom_call" | custom-call | tf_op jit(solution)/shard_map/gather_gain/pallas_call | solution.py:438
  65.2 0.7 %reshape.11 = f32[4,768]{1,0:T(4,128)} reshape(f32[4,4,2,96]{3,2,1,0:T(2,128)S(1)} %copy.6) | data formatting | bytes 24576 | tf_op jit(solution)/shard_map/reshape | solution.py:474
  65.9 0.6 copy.8
  (2 shorter events, 0.0 us)
